TPU v7x, 128 devices: a whole 4x4x4 slice. The times are simulated.
128 devices in a mesh: dp: 4 (over x), outer: 16 (over z, y), inner: 2 (over core).
Axes of the slice: x: 4, y: 4, z: 4, core: 2. Of those that a mesh axis runs over, the one named last changes fastest.
Arguments:
- queries: bfloat16 [4, 4096, 1024], P('dp', ('outer', 'inner')), may hold values from -6 to 6
- keys: bfloat16 [4, 4096, 2, 1024], P('dp', ('outer', 'inner')), may hold values from -6 to 6
- values: bfloat16 [4, 4096, 2, 1024], P('dp', ('outer', 'inner')), may hold values from -6 to 6
- betas: float32 [4, 8, 2, 4096], P('dp', None, None, ('outer', 'inner')), may hold values from 0.3 to 1.6
- grad_out: bfloat16 [4, 4096, 1024], P('dp', ('outer', 'inner')), may hold values from -16 to 16
- gain: float32 [1024], replicated, may hold values from 0.1 to 1.9
Outputs:
- grad_queries: bfloat16 [4, 4096, 1024], P('dp', ('outer', 'inner'))
- grad_keys: bfloat16 [4, 4096, 2, 1024], P('dp', ('outer', 'inner'))
- grad_values: bfloat16 [4, 4096, 2, 1024], P('dp', ('outer', 'inner'))
- gain_grad: float32 [1024], replicated
All inputs are finite; a program needn't handle non-finite values.
Results may differ from a plain program's by a relative error of at most 0.001.
Values sent between devices are 32-bit elements; how exact they have to be, the bound alone decides.
A program may use at most 128 MiB of HBM per device.

v0:
```python
import math
import jax
import jax.numpy as jnp
from jax import lax
from jax.sharding import PartitionSpec as P

HEADS = 8
HEAD_DIM = 128
STRETCH = 64
EXACT = lax.Precision.HIGHEST
EPS_KEY = 1e-06
EPS_OUT = 1e-05


def passed_along(block, axis, distance):
    devices = range(lax.axis_size(axis))
    route = [(i - distance, i) for i in devices if i - distance in devices]
    return lax.ppermute(block, axis, route)


def spread(value, axis, source):
    kept = jnp.where(lax.axis_index(axis) == source, value, 0).astype(value.dtype)
    return lax.psum(kept, axis)


def prefix(shard, axis, combine, identity, reverse):
    size, here = (lax.axis_size(axis), lax.axis_index(axis))
    everything = lax.all_gather(shard, axis)
    start = jnp.broadcast_to(jnp.asarray(identity, shard.dtype), shard.shape)

    def step(k, before):
        at = size - 1 - k if reverse else k
        reached = at > here if reverse else at < here
        new = combine(before, everything[at])
        return jnp.where(reached, new, before)

    return lax.fori_loop(0, size, step, start)


def product(spec, left, right):
    return jnp.einsum(spec, left, right, precision=EXACT, preferred_element_type=jnp.float32)


def unit_rows(raw):
    scale_inv = lax.rsqrt(jnp.sum(raw * raw, axis=-1, keepdims=True) + EPS_KEY)
    return (raw * scale_inv, scale_inv)


def unit_back(unit, scale_inv, grad):
    return scale_inv * (grad - unit * jnp.sum(unit * grad, axis=-1, keepdims=True))


def compose(earlier, later):
    through = product("mhij,hjk->mhik", earlier, later[0])
    return through + jnp.stack([jnp.zeros_like(later[1]), later[1]])


def stretch_factors(key_blk, value_blk, rate_blk, strict, eye_refl, eye_head):
    head_dim = key_blk.shape[2]
    gram = product("hrd,hsd->hrs", key_blk, key_blk)
    lower_mat = eye_refl + rate_blk[:, :, None] * gram * strict
    rhs = jnp.concatenate(
        [rate_blk[:, :, None] * key_blk, rate_blk[:, :, None] * value_blk], axis=2
    )
    solved = jax.scipy.linalg.solve_triangular(lower_mat, rhs, lower=True)
    w_mat = solved[:, :, :head_dim]
    t_vals = solved[:, :, head_dim:]
    transit = eye_head - product("hrd,hre->hde", w_mat, key_blk)
    return (lower_mat, w_mat, t_vals, transit)


def forward_nested(own_map, identity):
    count = lax.axis_size("inner")
    first = lax.axis_index("inner") == 0
    acc_map = identity
    sent = compose(acc_map, own_map)
    got = passed_along(sent, "inner", 1)
    acc_map = jnp.stack([jnp.where(first, identity[0], got[0]), got[1]])
    group_map = spread(compose(acc_map, own_map), "inner", count - 1)
    before = prefix(group_map, "outer", compose, identity, False)
    return compose(before, acc_map)


def backward_nested(own_map, identity):
    count = lax.axis_size("inner")
    final = lax.axis_index("inner") == count - 1
    acc_map = identity
    sent = compose(acc_map, own_map)
    got = passed_along(sent, "inner", -1)
    acc_map = jnp.stack([jnp.where(final, identity[0], got[0]), got[1]])
    group_map = spread(compose(acc_map, own_map), "inner", 0)
    after = prefix(group_map, "outer", compose, identity, True)
    return compose(after, acc_map)


def on_device(queries, keys, values, betas, grad_out, gain):
    length_here = queries.shape[1]
    heads = HEADS
    head_dim = HEAD_DIM
    span = STRETCH
    refl = 2 * span
    count = length_here // span
    query_raw = (
        queries[0].astype(jnp.float32).reshape(length_here, heads, head_dim).transpose(1, 0, 2)
    )
    key_raw = (
        keys[0]
        .astype(jnp.float32)
        .reshape(length_here, 2, heads, head_dim)
        .transpose(2, 0, 1, 3)
        .reshape(heads, 2 * length_here, head_dim)
    )
    value_all = (
        values[0]
        .astype(jnp.float32)
        .reshape(length_here, 2, heads, head_dim)
        .transpose(2, 0, 1, 3)
        .reshape(heads, 2 * length_here, head_dim)
    )
    rate_all = betas[0].transpose(0, 2, 1).reshape(heads, 2 * length_here)
    cotan_all = (
        grad_out[0].astype(jnp.float32).reshape(length_here, heads, head_dim).transpose(1, 0, 2)
    )
    gains = gain.reshape(heads, head_dim)
    query_n, query_inv = unit_rows(query_raw)
    key_n, key_inv = unit_rows(key_raw)
    token_ids = lax.broadcasted_iota(jnp.int32, (span, refl), 0)
    refl_ids = lax.broadcasted_iota(jnp.int32, (span, refl), 1)
    read_mask = (refl_ids <= 2 * token_ids + 1).astype(jnp.float32)
    row_ids = lax.broadcasted_iota(jnp.int32, (refl, refl), 0)
    col_ids = lax.broadcasted_iota(jnp.int32, (refl, refl), 1)
    strict = (col_ids < row_ids).astype(jnp.float32)
    eye_refl = jnp.eye(refl, dtype=jnp.float32)
    eye_head = jnp.eye(head_dim, dtype=jnp.float32)
    identity = jnp.stack(
        [
            jnp.broadcast_to(eye_head, (heads, head_dim, head_dim)),
            jnp.zeros((heads, head_dim, head_dim), jnp.float32),
        ]
    )

    def refl_rows(array, block_id):
        return array[:, block_id * refl : (block_id + 1) * refl]

    def token_rows(array, block_id):
        return array[:, block_id * span : (block_id + 1) * span]

    stash = []
    block_map = identity
    for block_id in range(count):
        key_blk = refl_rows(key_n, block_id)
        factor_set = stretch_factors(
            key_blk,
            refl_rows(value_all, block_id),
            refl_rows(rate_all, block_id),
            strict,
            eye_refl,
            eye_head,
        )
        offset = product("hrv,hre->hve", factor_set[2], key_blk)
        block_map = compose(block_map, jnp.stack([factor_set[3], offset]))
        stash.append(factor_set)

    def factors_of(block_id):
        return stash[block_id]

    state = forward_nested(block_map, identity)[1]
    records = []
    adjoint_maps = []
    gain_sum = jnp.zeros((heads, head_dim), jnp.float32)
    for block_id in range(count):
        lower_mat, w_mat, t_vals, transit = factors_of(block_id)
        key_blk = refl_rows(key_n, block_id)
        query_blk = token_rows(query_n, block_id)
        cotan_blk = token_rows(cotan_all, block_id)
        update = t_vals - product("hrk,hvk->hrv", w_mat, state)
        scores = product("htd,hrd->htr", query_blk, key_blk) * read_mask
        output = product("htk,hvk->htv", query_blk, state) + product("htr,hrv->htv", scores, update)
        scale_inv = lax.rsqrt(jnp.mean(output * output, axis=2, keepdims=True) + EPS_OUT)
        normed = output * scale_inv
        scaled = cotan_blk * gains[:, None, :]
        d_out = scale_inv * (scaled - normed * jnp.mean(normed * scaled, axis=2, keepdims=True))
        gain_sum = gain_sum + jnp.sum(cotan_blk * normed, axis=1)
        source = product("htv,htk->hvk", d_out, query_blk - product("htr,hrk->htk", scores, w_mat))
        records.append((state, update, scores, d_out))
        adjoint_maps.append(jnp.stack([jnp.swapaxes(transit, 1, 2), source]))
        state = state + product("hrv,hrk->hvk", update, key_blk)
    adjoint_block = identity
    for block_id in reversed(range(count)):
        adjoint_block = compose(adjoint_block, adjoint_maps[block_id])
    adjoint = backward_nested(adjoint_block, identity)[1]
    grad_q_parts = [None] * count
    grad_k_parts = [None] * count
    grad_v_parts = [None] * count
    for block_id in reversed(range(count)):
        lower_mat, w_mat, t_vals, transit = factors_of(block_id)
        start_state, update, scores, d_out = records[block_id]
        key_blk = refl_rows(key_n, block_id)
        query_blk = token_rows(query_n, block_id)
        rate_blk = refl_rows(rate_all, block_id)
        d_update = product("htr,htv->hrv", scores, d_out) + product(
            "hrk,hvk->hrv", key_blk, adjoint
        )
        solved = jax.scipy.linalg.solve_triangular(lower_mat, d_update, trans=1, lower=True)
        d_target = rate_blk[:, :, None] * solved
        d_scores = product("htv,hrv->htr", d_out, update) * read_mask
        grad_q_parts[block_id] = product("htv,hvk->htk", d_out, start_state) + product(
            "htr,hrk->htk", d_scores, key_blk
        )
        d_gram = -product("hrv,hsv->hrs", d_target, update) * strict
        grad_k_parts[block_id] = (
            product("hrv,hvk->hrk", update, adjoint)
            + product("htr,htk->hrk", d_scores, query_blk)
            - product("hrv,hvk->hrk", d_target, start_state)
            + product("hrs,hsk->hrk", d_gram + jnp.swapaxes(d_gram, 1, 2), key_blk)
        )
        grad_v_parts[block_id] = d_target
        adjoint = (
            adjoint
            + product("htv,htk->hvk", d_out, query_blk)
            - product("hrv,hrk->hvk", d_target, key_blk)
        )
    grad_qn = jnp.concatenate(grad_q_parts, axis=1)
    grad_kn = jnp.concatenate(grad_k_parts, axis=1)
    grad_val = jnp.concatenate(grad_v_parts, axis=1)
    grad_q = unit_back(query_n, query_inv, grad_qn)
    grad_k = unit_back(key_n, key_inv, grad_kn)
    grad_q = (
        grad_q.transpose(1, 0, 2).reshape(1, length_here, heads * head_dim).astype(jnp.bfloat16)
    )
    grad_k = (
        grad_k.reshape(heads, length_here, 2, head_dim)
        .transpose(1, 2, 0, 3)
        .reshape(1, length_here, 2, heads * head_dim)
        .astype(jnp.bfloat16)
    )
    grad_val = (
        grad_val.reshape(heads, length_here, 2, head_dim)
        .transpose(1, 2, 0, 3)
        .reshape(1, length_here, 2, heads * head_dim)
        .astype(jnp.bfloat16)
    )
    total = lax.psum(gain_sum, ("dp", "outer", "inner"))
    tokens_all = length_here * lax.axis_size("dp") * lax.axis_size("outer") * lax.axis_size("inner")
    gain_grad = total.reshape(heads * head_dim) * (1.0 / math.sqrt(tokens_all))
    return (grad_q, grad_k, grad_val, gain_grad)


def solution(mesh):
    return jax.shard_map(
        on_device,
        mesh=mesh,
        in_specs=(
            P("dp", ("outer", "inner"), None),
            P("dp", ("outer", "inner"), None, None),
            P("dp", ("outer", "inner"), None, None),
            P("dp", None, None, ("outer", "inner")),
            P("dp", ("outer", "inner"), None),
            P(),
        ),
        out_specs=(
            P("dp", ("outer", "inner"), None),
            P("dp", ("outer", "inner"), None, None),
            P("dp", ("outer", "inner"), None, None),
            P(),
        ),
        check_vma=False,
    )
```

profile of v0, /device:TPU:1, one launch (start us, length us, event | category | flops | bytes accessed | tf_op | source)
XLA Modules:
  0.0 764.0 jit_solution(11340195129437190525)
XLA Ops:
  13.8 79.8 %custom-call.9 = f32[8,1,128,128]{2,3,1,0:T(8,128)} custom-call(f32[8,1,128,128]{3,2,1,0:T(8,128)S(1)} %fusion.54), custom_call_target="InvertDiagBlocksLowerTriangular" | custom-call | tf_op jit(solution)/shard_map/jit(_solve_triangular)/vmap()/triangular_solve | solution.py:65
  103.9 79.4 %custom-call.8 = f32[8,1,128,128]{2,3,1,0:T(8,128)} custom-call(f32[8,1,128,128]{3,2,1,0:T(8,128)S(1)} %fusion.59), custom_call_target="InvertDiagBlocksLowerTriangular" | custom-call | tf_op jit(solution)/shard_map/jit(_solve_triangular)/vmap()/triangular_solve | solution.py:65
  183.3 2.4 fusion.69
  187.8 2.4 fusion.38
  196.4 3.9 collective-permute-done
  201.6 3.4 fusion.47
  205.1 28.1 %all-reduce.14.cloned.1.call-done = f32[1,2,8,128,128]{4,3,2,1,0:T(8,128)} async-done(((f32[1,2,8,128,128]{4,3,2,1,0:T(8,128)}), f32[1,2,8,128,128]{4,3,2,1,0:T(8,128)}) %all-reduce.14.cloned.1.call-update) | async-done | bytes 1048592 | tf_op jit(solution)/shard_map/psum | solution.py:23
  244.8 2.4 convolution_subtract_fusion.7
  247.2 100.7 %all-gather.3.cloned.1.call-done = f32[16,2,8,128,128]{4,3,2,1,0:T(8,128)} async-done(((f32[1,2,8,128,128]{4,3,2,1,0:T(8,128)}), f32[16,2,8,128,128]{4,3,2,1,0:T(8,128)}) %all-gather.3.cloned.1.call-update) | async-done | bytes 16777232 | tf_op jit(solution)/shard_map/all_gather | solution.py:28
  347.9 89.7 %while.28 = (s32[]{:T(128)}, f32[2,8,128,128]{2,3,1,0:T(8,128)}, s32[]{:T(128)}, f32[16,2,8,128,128]{4,3,2,1,0:T(8,128)}, s32[]{:T(128)}, /*index=5*/s32[]{:T(128)}, s32[]{}) while((s32[]{:T(128)}, f32[2,8,128,128]{2,3,1,0:T(8,128)}, s32[]{:T(128)}, f32[16,2,8,128,128]{4,3,2,1,0:T(8,128)}, s32[]{:T(128)}, /*index=5*/s32[]{:T(128)}, s32[]{}) %tuple.94), condition=%wide.region_4.6_spmd, body=%wide.region_3.5_spmd.sunk | while | flops 403177472 | bytes 8389227 | solution.py:37
  350.4 3.1 fusion.235
  356.0 3.1 fusion.235
  361.6 3.1 fusion.235
  367.2 3.1 fusion.235
  372.8 3.1 fusion.235
  378.4 3.1 fusion.235
  383.9 3.1 fusion.235
  389.5 3.1 fusion.235
  395.1 3.1 fusion.235
  400.7 3.1 fusion.235
  406.3 3.1 fusion.235
  411.9 3.1 fusion.235
  417.4 3.1 fusion.235
  423.0 3.1 fusion.235
  428.6 3.1 fusion.235
  434.2 3.1 fusion.235
  437.7 3.5 convolution_bitcast_fusion.5
  442.3 2.6 convolution_subtract_fusion.3
  445.9 2.6 convolution_subtract_fusion.2
  448.5 2.2 fusion.148
  465.1 2.7 collective-permute-start.1
  467.8 2.2 collective-permute-done.1
  473.9 25.0 %all-reduce.16.cloned.1.call-done = f32[1,2,8,128,128]{4,3,2,1,0:T(8,128)} async-done(((f32[1,2,8,128,128]{4,3,2,1,0:T(8,128)}), f32[1,2,8,128,128]{4,3,2,1,0:T(8,128)}) %all-reduce.16.cloned.1.call-update) | async-done | bytes 1048592 | tf_op jit(solution)/shard_map/psum | solution.py:23
  509.4 6.4 fusion.65
  517.5 68.1 %psum.23 = f32[8,128]{1,0:T(8,128)S(1)} all-reduce(f32[8,128]{1,0:T(8,128)S(1)} %add.275), channel_id=1, replica_groups=mesh['dp'=4,'outer'=16,'inner'=2] {'dp','outer','inner'}, use_global_device_ids=true, to_apply=%region_16.19 | all-reduce | flops 1024 | bytes 8192 | tf_op jit(solution)/shard_map/psum | solution.py:243
  586.2 2.7 fusion.171
  589.0 2.9 fusion.172
  591.9 2.9 fusion.140
  594.8 2.8 fusion.144
  597.6 17.5 %all-gather.5.cloned.1.call-done = f32[16,2,8,128,128]{4,3,2,1,0:T(8,128)} async-done(((f32[1,2,8,128,128]{4,3,2,1,0:T(8,128)}), f32[16,2,8,128,128]{4,3,2,1,0:T(8,128)}) %all-gather.5.cloned.1.call-update) | async-done | bytes 16777232 | tf_op jit(solution)/shard_map/all_gather | solution.py:28
  615.1 56.1 %while.29 = (s32[]{:T(128)}, f32[2,8,128,128]{2,3,1,0:T(8,128)S(1)}, s32[]{:T(128)}, f32[16,2,8,128,128]{4,3,2,1,0:T(8,128)}, s32[]{:T(128)}, /*index=5*/s32[]{:T(128)}, s32[]{:T(128)}, s32[]{:T(128)}, s32[]{}) while((s32[]{:T(128)}, f32[2,8,128,128]{2,3,1,0:T(8,128)S(1)}, s32[]{:T(128)}, f32[16,2,8,128,128]{4,3,2,1,0:T(8,128)}, ...), condition=%wide.region_12.14_spmd, body=%wide.region_11.13_spmd.sunk | while | flops 403177472 | bytes 8388781 | solution.py:37
  671.3 3.1 convolution_bitcast_fusion.2
  674.4 2.8 convolution_add_fusion.5
  679.9 3.0 convolution_negate_fusion
  685.1 2.4 convolution_add_fusion.3
  687.6 2.5 fusion.168
  693.5 3.1 convolution_negate_fusion.1
  711.1 44.5 %fusion.68 = bf16[128,2,8,128]{3,1,0,2:T(2,128)(2,1)S(1)} fusion(f32[8,128,2,128]{3,2,1,0:T(2,128)S(1)} %bitcast.296, f32[8,128,2]{2,1,0:T(8,128)} %copy.214, f32[128,2,8,128]{3,2,1,0:T(8,128)} %copy-done.14), kind=kOutput, calls=%fused_computation.98 | output fusion | flops 1837183 | bytes 2629632 | tf_op jit(solution)/shard_map/mul | solution.py:50
  (283 shorter events, 190.1 us)
Async XLA Ops:
  7.2 226.0 %all-reduce.14.cloned.1.call-start = ((), (), s32[]{:S(2)}) async-start(), calls=%async_computation | async-start | bytes 2097152 | tf_op jit(solution)/shard_map/psum | solution.py:23
  8.5 3.7 copy-start.14
  99.0 144.5 %copy-start.12 = (f32[8,128,256]{2,1,0:T(8,128)}, f32[8,128,256]{2,1,0:T(8,128)S(1)}, u32[]{:S(2)}) copy-start(f32[8,128,256]{2,1,0:T(8,128)S(1)} %fusion.73) | copy-start | bytes 3145732
  185.7 1.0 copy-start.13
  186.7 8.4 %copy-start.20 = (f32[8,128,128,1]{2,1,0,3:T(8,128)}, f32[8,128,128,1]{2,1,0,3:T(8,128)S(1)}, u32[]{:S(2)}) copy-start(f32[8,128,128,1]{2,1,0,3:T(8,128)S(1)} %fusion.55) | copy-start | bytes 1572868
  187.8 45.6 %copy-start.5 = (f32[1,8,128,128]{3,2,1,0:T(8,128)}, f32[1,8,128,128]{3,2,1,0:T(8,128)S(1)}, u32[]{:S(2)}) copy-start(f32[1,8,128,128]{3,2,1,0:T(8,128)S(1)} %stack_broadcast_in_dim.7) | copy-start | bytes 1572868
  192.2 1.0 copy-start.17
  193.2 3.3 copy-start.23
  195.1 5.2 collective-permute-start
  201.6 31.7 %copy-start.22 = (f32[1,8,128,128]{3,2,1,0:T(8,128)}, f32[1,8,128,128]{3,2,1,0:T(8,128)S(1)}, u32[]{:S(2)}) copy-start(f32[1,8,128,128]{3,2,1,0:T(8,128)S(1)} %get-tuple-element.266) | copy-start | bytes 1572868
  205.0 142.9 %all-gather.3.cloned.1.call-start = ((), (), s32[]{:S(2)}) async-start(), calls=%async_computation.1 | async-start | bytes 17825792 | tf_op jit(solution)/shard_map/all_gather | solution.py:28
  233.2 265.7 %all-reduce.16.cloned.1.call-start = ((), (), s32[]{:S(2)}) async-start(), calls=%async_computation.2 | async-start | bytes 2097152 | tf_op jit(solution)/shard_map/psum | solution.py:23
  239.9 1.4 copy-start.34
  240.0 4.9 copy-start.32
  241.3 3.6 copy-start.4
  242.4 209.9 %copy-start.25 = (f32[8,64,128]{2,1,0:T(8,128)}, f32[8,64,128]{2,1,0:T(8,128)S(1)}, u32[]{:S(2)}) copy-start(f32[8,64,128]{2,1,0:T(8,128)S(1)} %convolution_multiply_fusion.5) | copy-start | bytes 786436
  243.5 1.3 copy-start.26
  437.7 21.0 %copy-start.31 = (f32[8,64,128]{2,1,0:T(8,128)S(1)}, f32[8,64,128]{2,1,0:T(8,128)}, u32[]{:S(2)}) copy-start(f32[8,64,128]{2,1,0:T(8,128)} %convolution_subtract_fusion.7) | copy-start | bytes 786436
  437.7 22.0 %copy-start.6 = (f32[1,8,128,128]{3,2,1,0:T(8,128)S(1)}, f32[1,8,128,128]{3,2,1,0:T(8,128)}, u32[]{:S(2)}) copy-start(f32[1,8,128,128]{3,2,1,0:T(8,128)} %copy-done.5) | copy-start | bytes 1572868
  437.7 22.0 %copy-start.21 = (f32[8,128,128,1]{2,1,0,3:T(8,128)S(1)}, f32[8,128,128,1]{2,1,0,3:T(8,128)}, u32[]{:S(2)}) copy-start(f32[8,128,128,1]{2,1,0,3:T(8,128)} %copy-done.20) | copy-start | bytes 1572868
  437.7 23.2 %copy-start.30 = (f32[8,64,128]{2,1,0:T(8,128)S(1)}, f32[8,64,128]{2,1,0:T(8,128)}, u32[]{:S(2)}) copy-start(f32[8,64,128]{2,1,0:T(8,128)} %convolution_subtract_fusion.6) | copy-start | bytes 786436
  437.7 24.2 %copy-start.19 = (f32[8,128,128,1]{2,1,0,3:T(8,128)S(1)}, f32[8,128,128,1]{2,1,0,3:T(8,128)}, u32[]{:S(2)}) copy-start(f32[8,128,128,1]{2,1,0,3:T(8,128)} %fusion.50) | copy-start | bytes 1572868
  442.3 64.9 %copy-start = (f32[8,128,128]{2,1,0:T(8,128)}, f32[8,128,128]{2,1,0:T(8,128)S(1)}, u32[]{:S(2)}) copy-start(f32[8,128,128]{2,1,0:T(8,128)S(1)} %fusion.88) | copy-start | bytes 1572868
  444.9 60.1 %copy-start.2 = (f32[8,128,128]{2,1,0:T(8,128)}, f32[8,128,128]{2,1,0:T(8,128)S(1)}, u32[]{:S(2)}) copy-start(f32[8,128,128]{2,1,0:T(8,128)S(1)} %convolution_subtract_fusion.3) | copy-start | bytes 1572868
  445.9 7.1 copy-start.11
  448.5 3.8 copy-start.7
  458.6 2.3 copy-start.18
  465.1 4.9 collective-permute-start.1
  470.0 1.0 copy-start.27
  471.0 0.8 copy-start.9
  473.9 141.2 %all-gather.5.cloned.1.call-start = ((), (), s32[]{:S(2)}) async-start(), calls=%async_computation.3 | async-start | bytes 17825792 | tf_op jit(solution)/shard_map/all_gather | solution.py:28
  503.7 0.7 copy-start.29
  507.2 1.7 copy-start.28
  671.2 22.3 %copy-start.3 = (f32[8,128,128]{2,1,0:T(8,128)S(1)}, f32[8,128,128]{2,1,0:T(8,128)}, u32[]{:S(2)}) copy-start(f32[8,128,128]{2,1,0:T(8,128)} %copy-done.2) | copy-start | bytes 1572868
  671.2 29.2 %copy-start.1 = (f32[8,128,128]{2,1,0:T(8,128)S(1)}, f32[8,128,128]{2,1,0:T(8,128)}, u32[]{:S(2)}) copy-start(f32[8,128,128]{2,1,0:T(8,128)} %copy-done) | copy-start | bytes 1572868
  674.3 13.2 %copy-start.16 = (f32[2,8,128,128]{3,2,1,0:T(8,128)}, f32[2,8,128,128]{3,2,1,0:T(8,128)S(1)}, u32[]{:S(2)}) copy-start(f32[2,8,128,128]{3,2,1,0:T(8,128)S(1)} %convolution_bitcast_fusion.2) | copy-start | bytes 3145732
  674.4 29.1 %copy-start.8 = (f32[8,128,128]{2,1,0:T(8,128)S(1)}, f32[8,128,128]{2,1,0:T(8,128)}, u32[]{:S(2)}) copy-start(f32[8,128,128]{2,1,0:T(8,128)} %copy-done.7) | copy-start | bytes 1572868
  674.4 29.1 %copy-start.10 = (f32[1,8,128,128]{3,2,1,0:T(8,128)S(1)}, f32[1,8,128,128]{3,2,1,0:T(8,128)}, u32[]{:S(2)}) copy-start(f32[1,8,128,128]{3,2,1,0:T(8,128)} %copy-done.9) | copy-start | bytes 1572868
  674.4 33.0 %copy-start.33 = (f32[128,128]{1,0:T(8,128)S(1)}, f32[128,128]{1,0:T(8,128)}, u32[]{:S(2)}) copy-start(f32[128,128]{1,0:T(8,128)} %get-tuple-element.288) | copy-start | bytes 196612
  678.9 6.2 copy-start.15
  685.1 5.0 copy-start.24
Sparse Core Ops, SparseCore 0:
  205.1 28.0 all-reduce.13
  235.5 112.3 all-gather.2
  474.0 24.8 all-reduce.15
  500.9 114.1 all-gather.4
where the time goes:
time: 773 us; the launch traced here: 764 us
  other arithmetic  223 us (29%)
  matrix products  188 us (24%)
  waiting for transfers between devices  177 us (23%)
  local copies, waits for them, and re-layouts  85.9 us (11%)
  blocking collectives  68.1 us (9%)
  between operations  15 us (2%)
    dot_general x83, matrix products, product(): jnp.einsum(spec, left, right, precision=EXACT, preferred_element_type=jnp...  180 us
    another operation x3, other arithmetic, stretch_factors(): solved = jax.scipy.linalg.solve_triangular(lower_mat, rhs, lower=True)  159 us
    all_gather x2, waiting for transfers between devices, prefix(): everything = lax.all_gather(shard, axis)  118 us
    psum x1, blocking collectives, on_device(): total = lax.psum(gain_sum, ('dp', 'outer', 'inner'))  68.1 us
    psum x2, waiting for transfers between devices, spread(): return lax.psum(kept, axis)  53.1 us
    mul x2, other arithmetic, unit_back(): unit * jnp.sum(unit * grad, axis=-1, keepdims=True)  50.9 us
    slice x34, local copies, waits for them, and re-layouts, compose(): return through + jnp.stack([jnp.zeros_like(later[1]), later[1]])  34.6 us
    while x64, local copies, waits for them, and re-layouts  27 us
  transfers between devices with their start and end apart: 6, of which 6 were waited for; matrix products, arithmetic and copies ran while one was open for 6% of the time, Pallas kernels for 0%

commit v1 on v0

--- a/solution.py
+++ b/solution.py
@@ -240,7 +240,7 @@
         .reshape(1, length_here, 2, heads * head_dim)
         .astype(jnp.bfloat16)
     )
-    total = lax.psum(gain_sum, ("dp", "outer", "inner"))
+    total = lax.psum(lax.psum(gain_sum, "dp"), ("outer", "inner"))
     tokens_all = length_here * lax.axis_size("dp") * lax.axis_size("outer") * lax.axis_size("inner")
     gain_grad = total.reshape(heads * head_dim) * (1.0 / math.sqrt(tokens_all))
     return (grad_q, grad_k, grad_val, gain_grad)

time: 773 us -> 772 us (level)
    psum x1 -> x2, blocking collectives: 68.1 us -> 74.1 us  [on_device(): total = lax.psum(lax.psum(gain_sum, 'dp'), ('outer', 'inner'))]
where the time goes in v1:
time: 772 us; the launch traced here: 763 us
  other arithmetic  223 us (29%)
  matrix products  188 us (24%)
  waiting for transfers between devices  170 us (22%)
  local copies, waits for them, and re-layouts  85.9 us (11%)
  blocking collectives  74.1 us (10%)
  between operations  15 us (2%)
    dot_general x83, matrix products, product(): jnp.einsum(spec, left, right, precision=EXACT, preferred_element_type=jnp...  180 us
    another operation x3, other arithmetic, stretch_factors(): solved = jax.scipy.linalg.solve_triangular(lower_mat, rhs, lower=True)  159 us
    all_gather x2, waiting for transfers between devices, prefix(): everything = lax.all_gather(shard, axis)  111 us
    psum x2, blocking collectives, on_device(): total = lax.psum(lax.psum(gain_sum, 'dp'), ('outer', 'inner'))  74.1 us
    psum x2, waiting for transfers between devices, spread(): return lax.psum(kept, axis)  53.1 us
    mul x2, other arithmetic, unit_back(): unit * jnp.sum(unit * grad, axis=-1, keepdims=True)  50.8 us
    slice x34, local copies, waits for them, and re-layouts, compose(): return through + jnp.stack([jnp.zeros_like(later[1]), later[1]])  34.6 us
    while x64, local copies, waits for them, and re-layouts  27 us
  transfers between devices with their start and end apart: 6, of which 6 were waited for; matrix products, arithmetic and copies ran while one was open for 6% of the time, Pallas kernels for 0%

profile of v1, /device:TPU:1, one launch (start us, length us, event | category | flops | bytes accessed | tf_op | source)
XLA Modules:
  0.0 762.8 jit_solution(14330309725084646063)
XLA Ops:
  13.9 79.8 %custom-call.9 = f32[8,1,128,128]{2,3,1,0:T(8,128)} custom-call(f32[8,1,128,128]{3,2,1,0:T(8,128)S(1)} %fusion.54), custom_call_target="InvertDiagBlocksLowerTriangular" | custom-call | tf_op jit(solution)/shard_map/jit(_solve_triangular)/vmap()/triangular_solve | solution.py:65
  103.9 79.4 %custom-call.8 = f32[8,1,128,128]{2,3,1,0:T(8,128)} custom-call(f32[8,1,128,128]{3,2,1,0:T(8,128)S(1)} %fusion.59), custom_call_target="InvertDiagBlocksLowerTriangular" | custom-call | tf_op jit(solution)/shard_map/jit(_solve_triangular)/vmap()/triangular_solve | solution.py:65
  183.3 2.4 fusion.69
  187.8 2.4 fusion.38
  196.4 3.9 collective-permute-done
  201.6 3.4 fusion.47
  205.1 28.1 %all-reduce.14.cloned.1.call-done = f32[1,2,8,128,128]{4,3,2,1,0:T(8,128)} async-done(((f32[1,2,8,128,128]{4,3,2,1,0:T(8,128)}), f32[1,2,8,128,128]{4,3,2,1,0:T(8,128)}) %all-reduce.14.cloned.1.call-update) | async-done | bytes 1048592 | tf_op jit(solution)/shard_map/psum | solution.py:23
  244.9 2.4 convolution_subtract_fusion.7
  247.2 100.7 %all-gather.3.cloned.1.call-done = f32[16,2,8,128,128]{4,3,2,1,0:T(8,128)} async-done(((f32[1,2,8,128,128]{4,3,2,1,0:T(8,128)}), f32[16,2,8,128,128]{4,3,2,1,0:T(8,128)}) %all-gather.3.cloned.1.call-update) | async-done | bytes 16777232 | tf_op jit(solution)/shard_map/all_gather | solution.py:28
  347.9 89.9 %while.28 = (s32[]{:T(128)}, f32[2,8,128,128]{2,3,1,0:T(8,128)}, s32[]{:T(128)}, f32[16,2,8,128,128]{4,3,2,1,0:T(8,128)}, s32[]{:T(128)}, /*index=5*/s32[]{:T(128)}, s32[]{}) while((s32[]{:T(128)}, f32[2,8,128,128]{2,3,1,0:T(8,128)}, s32[]{:T(128)}, f32[16,2,8,128,128]{4,3,2,1,0:T(8,128)}, s32[]{:T(128)}, /*index=5*/s32[]{:T(128)}, s32[]{}) %tuple.94), condition=%wide.region_4.6_spmd, body=%wide.region_3.5_spmd.sunk | while | flops 403177472 | bytes 8389227 | solution.py:37
  350.4 3.1 fusion.235
  356.0 3.1 fusion.235
  361.6 3.1 fusion.235
  367.2 3.1 fusion.235
  372.8 3.1 fusion.235
  378.4 3.1 fusion.235
  384.0 3.1 fusion.235
  389.6 3.1 fusion.235
  395.2 3.1 fusion.235
  400.8 3.1 fusion.235
  406.4 3.1 fusion.235
  412.0 3.1 fusion.235
  417.6 3.1 fusion.235
  423.2 3.1 fusion.235
  428.8 3.1 fusion.235
  434.4 3.1 fusion.235
  437.9 3.5 convolution_bitcast_fusion.5
  442.5 2.6 convolution_subtract_fusion.3
  446.1 2.6 convolution_subtract_fusion.2
  448.7 2.2 fusion.148
  465.3 2.7 collective-permute-start.1
  474.1 25.0 %all-reduce.16.cloned.1.call-done = f32[1,2,8,128,128]{4,3,2,1,0:T(8,128)} async-done(((f32[1,2,8,128,128]{4,3,2,1,0:T(8,128)}), f32[1,2,8,128,128]{4,3,2,1,0:T(8,128)}) %all-reduce.16.cloned.1.call-update) | async-done | bytes 1048592 | tf_op jit(solution)/shard_map/psum | solution.py:23
  509.6 6.4 fusion.65
  517.7 9.3 %psum.30 = f32[8,128]{1,0:T(8,128)S(1)} all-reduce(f32[8,128]{1,0:T(8,128)S(1)} %add.277), channel_id=1, replica_groups=mesh['dp'=4,'outer'=16,'inner'=2] {'dp'}, use_global_device_ids=true, to_apply=%region_16.19 | all-reduce | flops 1024 | bytes 8192 | tf_op jit(solution)/shard_map/psum | solution.py:243
  527.0 64.9 %psum.31 = f32[8,128]{1,0:T(8,128)S(1)} all-reduce(f32[8,128]{1,0:T(8,128)S(1)} %psum.30), channel_id=1, replica_groups=mesh['dp'=4,'outer'=16,'inner'=2] {'outer','inner'}, use_global_device_ids=true, to_apply=%region_17.20 | all-reduce | flops 1024 | bytes 8192 | tf_op jit(solution)/shard_map/psum | solution.py:243
  592.5 2.8 fusion.171
  595.2 2.9 fusion.172
  598.1 2.9 fusion.140
  601.0 2.8 fusion.144
  603.8 10.2 %all-gather.5.cloned.1.call-done = f32[16,2,8,128,128]{4,3,2,1,0:T(8,128)} async-done(((f32[1,2,8,128,128]{4,3,2,1,0:T(8,128)}), f32[16,2,8,128,128]{4,3,2,1,0:T(8,128)}) %all-gather.5.cloned.1.call-update) | async-done | bytes 16777232 | tf_op jit(solution)/shard_map/all_gather | solution.py:28
  614.0 56.1 %while.29 = (s32[]{:T(128)}, f32[2,8,128,128]{2,3,1,0:T(8,128)S(1)}, s32[]{:T(128)}, f32[16,2,8,128,128]{4,3,2,1,0:T(8,128)}, s32[]{:T(128)}, /*index=5*/s32[]{:T(128)}, s32[]{:T(128)}, s32[]{:T(128)}, s32[]{}) while((s32[]{:T(128)}, f32[2,8,128,128]{2,3,1,0:T(8,128)S(1)}, s32[]{:T(128)}, f32[16,2,8,128,128]{4,3,2,1,0:T(8,128)}, ...), condition=%wide.region_12.14_spmd, body=%wide.region_11.13_spmd.sunk | while | flops 403177472 | bytes 8388781 | solution.py:37
  670.2 3.1 convolution_bitcast_fusion.2
  673.3 2.8 convolution_add_fusion.5
  678.9 3.0 convolution_negate_fusion
  684.1 2.4 convolution_add_fusion.3
  686.5 2.5 fusion.168
  692.5 3.0 convolution_negate_fusion.1
  710.1 44.4 %fusion.68 = bf16[128,2,8,128]{3,1,0,2:T(2,128)(2,1)S(1)} fusion(f32[8,128,2,128]{3,2,1,0:T(2,128)S(1)} %bitcast.296, f32[8,128,2]{2,1,0:T(8,128)} %copy.214, f32[128,2,8,128]{3,2,1,0:T(8,128)} %copy-done.14), kind=kOutput, calls=%fused_computation.98 | output fusion | flops 1837183 | bytes 2629632 | tf_op jit(solution)/shard_map/mul | solution.py:50
  (284 shorter events, 192.4 us)
Async XLA Ops:
  7.2 226.0 %all-reduce.14.cloned.1.call-start = ((), (), s32[]{:S(2)}) async-start(), calls=%async_computation | async-start | bytes 2097152 | tf_op jit(solution)/shard_map/psum | solution.py:23
  8.5 3.7 copy-start.14
  99.0 144.6 %copy-start.12 = (f32[8,128,256]{2,1,0:T(8,128)}, f32[8,128,256]{2,1,0:T(8,128)S(1)}, u32[]{:S(2)}) copy-start(f32[8,128,256]{2,1,0:T(8,128)S(1)} %fusion.73) | copy-start | bytes 3145732
  185.7 1.0 copy-start.13
  186.7 8.4 %copy-start.20 = (f32[8,128,128,1]{2,1,0,3:T(8,128)}, f32[8,128,128,1]{2,1,0,3:T(8,128)S(1)}, u32[]{:S(2)}) copy-start(f32[8,128,128,1]{2,1,0,3:T(8,128)S(1)} %fusion.55) | copy-start | bytes 1572868
  187.8 45.6 %copy-start.5 = (f32[1,8,128,128]{3,2,1,0:T(8,128)}, f32[1,8,128,128]{3,2,1,0:T(8,128)S(1)}, u32[]{:S(2)}) copy-start(f32[1,8,128,128]{3,2,1,0:T(8,128)S(1)} %stack_broadcast_in_dim.7) | copy-start | bytes 1572868
  192.2 1.0 copy-start.17
  193.2 3.3 copy-start.23
  195.1 5.2 collective-permute-start
  201.6 31.8 %copy-start.22 = (f32[1,8,128,128]{3,2,1,0:T(8,128)}, f32[1,8,128,128]{3,2,1,0:T(8,128)S(1)}, u32[]{:S(2)}) copy-start(f32[1,8,128,128]{3,2,1,0:T(8,128)S(1)} %get-tuple-element.266) | copy-start | bytes 1572868
  205.0 142.9 %all-gather.3.cloned.1.call-start = ((), (), s32[]{:S(2)}) async-start(), calls=%async_computation.1 | async-start | bytes 17825792 | tf_op jit(solution)/shard_map/all_gather | solution.py:28
  233.2 265.9 %all-reduce.16.cloned.1.call-start = ((), (), s32[]{:S(2)}) async-start(), calls=%async_computation.2 | async-start | bytes 2097152 | tf_op jit(solution)/shard_map/psum | solution.py:23
  239.9 1.4 copy-start.34
  240.0 4.9 copy-start.32
  241.3 3.6 copy-start.4
  242.4 210.1 %copy-start.25 = (f32[8,64,128]{2,1,0:T(8,128)}, f32[8,64,128]{2,1,0:T(8,128)S(1)}, u32[]{:S(2)}) copy-start(f32[8,64,128]{2,1,0:T(8,128)S(1)} %convolution_multiply_fusion.5) | copy-start | bytes 786436
  243.5 1.3 copy-start.26
  437.8 21.0 %copy-start.31 = (f32[8,64,128]{2,1,0:T(8,128)S(1)}, f32[8,64,128]{2,1,0:T(8,128)}, u32[]{:S(2)}) copy-start(f32[8,64,128]{2,1,0:T(8,128)} %convolution_subtract_fusion.7) | copy-start | bytes 786436
  437.9 22.0 %copy-start.6 = (f32[1,8,128,128]{3,2,1,0:T(8,128)S(1)}, f32[1,8,128,128]{3,2,1,0:T(8,128)}, u32[]{:S(2)}) copy-start(f32[1,8,128,128]{3,2,1,0:T(8,128)} %copy-done.5) | copy-start | bytes 1572868
  437.9 22.0 %copy-start.21 = (f32[8,128,128,1]{2,1,0,3:T(8,128)S(1)}, f32[8,128,128,1]{2,1,0,3:T(8,128)}, u32[]{:S(2)}) copy-start(f32[8,128,128,1]{2,1,0,3:T(8,128)} %copy-done.20) | copy-start | bytes 1572868
  437.9 23.2 %copy-start.30 = (f32[8,64,128]{2,1,0:T(8,128)S(1)}, f32[8,64,128]{2,1,0:T(8,128)}, u32[]{:S(2)}) copy-start(f32[8,64,128]{2,1,0:T(8,128)} %convolution_subtract_fusion.6) | copy-start | bytes 786436
  437.9 24.2 %copy-start.19 = (f32[8,128,128,1]{2,1,0,3:T(8,128)S(1)}, f32[8,128,128,1]{2,1,0,3:T(8,128)}, u32[]{:S(2)}) copy-start(f32[8,128,128,1]{2,1,0,3:T(8,128)} %fusion.50) | copy-start | bytes 1572868
  442.5 64.9 %copy-start = (f32[8,128,128]{2,1,0:T(8,128)}, f32[8,128,128]{2,1,0:T(8,128)S(1)}, u32[]{:S(2)}) copy-start(f32[8,128,128]{2,1,0:T(8,128)S(1)} %fusion.88) | copy-start | bytes 1572868
  445.1 60.1 %copy-start.2 = (f32[8,128,128]{2,1,0:T(8,128)}, f32[8,128,128]{2,1,0:T(8,128)S(1)}, u32[]{:S(2)}) copy-start(f32[8,128,128]{2,1,0:T(8,128)S(1)} %convolution_subtract_fusion.3) | copy-start | bytes 1572868
  446.1 7.1 copy-start.11
  448.7 3.8 copy-start.7
  458.8 2.3 copy-start.18
  465.3 4.9 collective-permute-start.1
  470.2 1.0 copy-start.27
  471.2 0.8 copy-start.9
  474.0 140.0 %all-gather.5.cloned.1.call-start = ((), (), s32[]{:S(2)}) async-start(), calls=%async_computation.3 | async-start | bytes 17825792 | tf_op jit(solution)/shard_map/all_gather | solution.py:28
  503.9 0.7 copy-start.29
  507.3 1.7 copy-start.28
  670.2 22.3 %copy-start.3 = (f32[8,128,128]{2,1,0:T(8,128)S(1)}, f32[8,128,128]{2,1,0:T(8,128)}, u32[]{:S(2)}) copy-start(f32[8,128,128]{2,1,0:T(8,128)} %copy-done.2) | copy-start | bytes 1572868
  670.2 29.2 %copy-start.1 = (f32[8,128,128]{2,1,0:T(8,128)S(1)}, f32[8,128,128]{2,1,0:T(8,128)}, u32[]{:S(2)}) copy-start(f32[8,128,128]{2,1,0:T(8,128)} %copy-done) | copy-start | bytes 1572868
  673.3 13.2 %copy-start.16 = (f32[2,8,128,128]{3,2,1,0:T(8,128)}, f32[2,8,128,128]{3,2,1,0:T(8,128)S(1)}, u32[]{:S(2)}) copy-start(f32[2,8,128,128]{3,2,1,0:T(8,128)S(1)} %convolution_bitcast_fusion.2) | copy-start | bytes 3145732
  673.3 29.0 %copy-start.8 = (f32[8,128,128]{2,1,0:T(8,128)S(1)}, f32[8,128,128]{2,1,0:T(8,128)}, u32[]{:S(2)}) copy-start(f32[8,128,128]{2,1,0:T(8,128)} %copy-done.7) | copy-start | bytes 1572868
  673.3 29.0 %copy-start.10 = (f32[1,8,128,128]{3,2,1,0:T(8,128)S(1)}, f32[1,8,128,128]{3,2,1,0:T(8,128)}, u32[]{:S(2)}) copy-start(f32[1,8,128,128]{3,2,1,0:T(8,128)} %copy-done.9) | copy-start | bytes 1572868
  673.3 33.0 %copy-start.33 = (f32[128,128]{1,0:T(8,128)S(1)}, f32[128,128]{1,0:T(8,128)}, u32[]{:S(2)}) copy-start(f32[128,128]{1,0:T(8,128)} %get-tuple-element.288) | copy-start | bytes 196612
  677.9 6.2 copy-start.15
  684.1 5.0 copy-start.24
Sparse Core Ops, SparseCore 0:
  205.1 28.0 all-reduce.13
  235.5 112.3 all-gather.2
  474.2 24.8 all-reduce.15
  501.1 112.9 all-gather.4
